TPU v7x, 32 devices: a whole 2x2x4 slice. The times are simulated.
32 devices in a mesh: groups: 2 (over x), gx: 16 (over z, y, core).
Axes of the slice: x: 2, y: 2, z: 4, core: 2. Of those that a mesh axis runs over, the one named last changes fastest.
Arguments:
- efield: float32 [3, 64, 64, 256], P(None, ('groups', 'gx')), parts along dimension 1, may hold values from -6 to 6
- hfield: float32 [3, 64, 64, 256], P(None, ('groups', 'gx')), parts along dimension 1, may hold values from -6 to 6
- material: int32 [64, 64, 256], P(('groups', 'gx')), parts along dimension 0, may hold values from 0 to 15
- mat_eps: float32 [16], replicated, may hold values from 1 to 4
- mat_sigma: float32 [16], replicated, may hold values from 0.05 to 1
- seg_owner: int32 [32768, 1], P(('groups', 'gx')), parts along dimension 0, may hold values from 0 to 15; in each aligned block of 1024 rows (0 to 1023, 1024 to 2047, ...) at most 128 rows name the same one
- seg_cell: int32 [32768], P(('groups', 'gx')), parts along dimension 0, may hold values from 0 to 32767
- chain_start: int32 [32768], P(('groups', 'gx')), parts along dimension 0, may hold values 0 or 1
- couple: float32 [3, 64, 32768], P(None, None, ('groups', 'gx')), parts along dimension 2, may hold values from -1.5 to 1.5
- voltage: float32 [64, 32768], P(None, ('groups', 'gx')), parts along dimension 1, may hold values from -6 to 6
- current: float32 [64, 32768], P(None, ('groups', 'gx')), parts along dimension 1, may hold values from -6 to 6
- induct_step: float32 [64, 64], replicated, may hold values from -0.04 to 0.8, as said below
- capac_step: float32 [64, 64], replicated, may hold values from -0.04 to 0.8, as said below
Outputs:
- efield_out: float32 [3, 64, 64, 256], P(None, ('groups', 'gx')), parts along dimension 1
- hfield_out: float32 [3, 64, 64, 256], P(None, ('groups', 'gx')), parts along dimension 1
- voltage_out: float32 [64, 32768], P(None, ('groups', 'gx')), parts along dimension 1
- current_out: float32 [64, 32768], P(None, ('groups', 'gx')), parts along dimension 1
There are 2 independent parts, one for each index of `groups`. A program takes and returns all parts, laid end to end along the dimension named above; an argument that names none is the same for every part. Nothing has to cross between parts.
Inputs may be any that keep to these rules, and one draw needn't show every extreme that they name: `seg_owner`: among the 1024 segments of one device, at most 128 name the same device. `seg_cell`: Row-major index over the 2 x 64 x 256 cells of that device's slab. `induct_step`: Symmetric. `capac_step`: Symmetric.
All inputs are finite; a program needn't handle non-finite values. No bound on the sum of `chain_start` on one device may be relied on, other than what follows from the above.
Results may differ from a plain program's by a relative error of at most 0.0001.
Values sent between devices are 32-bit elements; how exact they have to be, the bound alone decides.
A program may use at most 128 MiB of HBM per device.

v0:
```python
import functools

import jax
import jax.numpy as jnp
from jax import lax
from jax.experimental import pallas as pl
from jax.experimental.pallas import tpu as pltpu
from jax.sharding import PartitionSpec as P

STEPS = 4
COURANT = 0.55
MESH = pl.DeviceIdType.MESH
F32 = jnp.float32
BF16 = jnp.bfloat16
PAIRS = ((0, 0), (0, 1), (0, 2), (1, 1), (1, 2), (2, 2))
LANES = 128


def split(x):
    high = x.astype(BF16)
    return high, (x - high.astype(F32)).astype(BF16)


def dot(a, b):
    return jnp.dot(a, b, preferred_element_type=F32)


def dot_nt(a, b):
    return lax.dot_general(a, b, (((1,), (1,)), ((), ())), preferred_element_type=F32)


def iota(shape, dim):
    return lax.broadcasted_iota(jnp.int32, shape, dim)


def kernel(
    n,
    ny,
    e_in,
    h_in,
    material,
    mat_eps,
    mat_sigma,
    seg_owner,
    seg_cell,
    chain_start,
    couple,
    v_in,
    i_in,
    induct,
    capac,
    e_ref,
    h_ref,
    v_ref,
    i_ref,
    keep_ref,
    drive_ref,
    memb_ref,
    rank_ref,
    lc_ref,
    j_ref,
    ohz_ref,
    ohr_ref,
    spread_ref,
    m_ref,
    eg_ref,
    bout_ref,
    msg_out,
    msg_in,
    e_halo,
    h_halo,
    v_out,
    v_edge,
    i_out,
    i_edge,
    msg_ssem,
    msg_rsem,
    e_ssem,
    e_rsem,
    h_ssem,
    h_rsem,
    v_ssem,
    v_rsem,
    i_ssem,
    i_rsem,
):
    me = lax.axis_index("gx")
    _, rows, nz = e_in.shape
    cond, seg = v_in.shape
    cap = msg_in.shape[-1]
    slots = n * cap
    first, last = me == 0, me == n - 1
    not_first, not_last = me > 0, me < n - 1

    def partner(k):
        result, bit = 0, 1
        while bit < n:
            digit = (me // bit) % 2
            result = result + (((1 - digit) if (k & bit) else digit) * bit)
            bit *= 2
        return result

    partners = [partner(k) for k in range(n)]

    barrier = pltpu.get_barrier_semaphore()
    for k in range(1, n):
        pl.semaphore_signal(barrier, inc=1, device_id={"gx": partners[k]}, device_id_type=MESH)

    def to_partner(index, k):
        return pltpu.make_async_remote_copy(
            src_ref=msg_out.at[index, k],
            dst_ref=msg_in.at[index, k],
            send_sem=msg_ssem.at[index],
            recv_sem=msg_rsem.at[index],
            device_id={"gx": partners[k]},
            device_id_type=MESH,
        )

    def send_messages(index):
        for k in range(1, n):
            to_partner(index, k).start()
        msg_in[index, 0] = msg_out[index, 0]

    def wait_messages(index):
        part = msg_in.at[index, pl.ds(1, n - 1)]
        pltpu.make_async_copy(part, part, msg_rsem.at[index]).wait()

    def wait_sent(index):
        part = msg_out.at[index, pl.ds(1, n - 1)]
        pltpu.make_async_copy(part, part, msg_ssem.at[index]).wait()

    def to_neighbour(source, target, ssem, rsem, step, direction):
        return pltpu.make_async_remote_copy(
            src_ref=source,
            dst_ref=target.at[step],
            send_sem=ssem.at[step],
            recv_sem=rsem.at[step],
            device_id={"gx": (me + direction + n) % n},
            device_id_type=MESH,
        )

    def e_copy(source, step):
        return to_neighbour(
            source.at[pl.ds(1, 2), pl.ds(0, ny)], e_halo, e_ssem, e_rsem, step, -1
        )

    def h_copy(step):
        return to_neighbour(
            h_ref.at[pl.ds(1, 2), pl.ds(rows - ny, ny)], h_halo, h_ssem, h_rsem, step, 1
        )

    def v_copy(step):
        return to_neighbour(v_out.at[step], v_edge, v_ssem, v_rsem, step, -1)

    def i_copy(step):
        return to_neighbour(i_out.at[step], i_edge, i_ssem, i_rsem, step, 1)

    link_behind = 1.0 - chain_start[...].astype(F32)
    eye = iota((cond, v_edge.shape[-1]), 0) == iota((cond, v_edge.shape[-1]), 1)
    seg_lane = iota((1, seg), 1)

    def pack_edge(column):
        row = jnp.sum(jnp.where(eye, column, 0.0), axis=0, keepdims=True)
        return jnp.broadcast_to(row, (8, row.shape[1]))

    def unpack_edge(block):
        return jnp.sum(jnp.where(eye, block[0:1], 0.0), axis=1, keepdims=True)

    def times(matrix, x):
        mh, ml = split(matrix)
        xh, xl = split(x)
        return dot(mh, xh) + dot(mh, xl) + dot(ml, xh)

    def to_slots(values):
        product = jnp.concatenate([values] * n, axis=0) * memb_ref[...]
        high, low = split(product)
        result = dot_nt(high, rank_ref[...]) + dot_nt(low, rank_ref[...])
        return result.reshape(n, 8, cap)

    def from_slots(block):
        high, low = split(block.reshape(n * 8, cap))
        spread = dot(high, rank_ref[...]) + dot(low, rank_ref[...])
        return jnp.sum((spread * memb_ref[...]).reshape(n, 8, seg), axis=0)

    def as_rows(index):
        return jnp.concatenate([msg_in[index, k] for k in range(n)], axis=1)

    def send_volt(volt, step):
        v_out[step] = pack_edge(volt[:, 0:1] * link_behind[:, 0:1])

        @pl.when(not_first)
        def _():
            v_copy(step).start()

    def pending_current(current, volt, step):
        @pl.when(not_last)
        def _():
            v_copy(step).wait_recv()

        edge = unpack_edge(v_edge[step])
        ahead = pltpu.roll(volt * link_behind, seg - 1, 1)
        ahead = jnp.where(seg_lane == seg - 1, edge, ahead)
        pending = current - times(induct[...], ahead - volt)
        j_ref[...] = pending
        values = [jnp.sum(couple[c] * pending, axis=0, keepdims=True) for c in range(3)]
        zeros = jnp.zeros((1, seg), F32)
        bout_ref[...] = to_slots(jnp.concatenate([zeros] * 3 + values + [zeros] * 2, axis=0))

    row_of = iota((rows, 1), 0)
    y_of = row_of % ny
    z_of = iota((1, nz), 1)

    def ahead_y(x):
        return jnp.where(y_of == ny - 1, 0.0, pltpu.roll(x, rows - 1, 0))

    def ahead_z(x):
        return jnp.where(z_of == nz - 1, 0.0, pltpu.roll(x, nz - 1, 1))

    def behind_y(x):
        return jnp.where(y_of == 0, 0.0, pltpu.roll(x, 1, 0))

    def behind_z(x):
        return jnp.where(z_of == 0, 0.0, pltpu.roll(x, 1, 1))

    def magnetic(efield, hfield, step):
        @pl.when(not_last)
        def _():
            e_copy(e_in, step).wait_recv()

        if step > 0:

            @pl.when(not_last)
            def _():
                h_copy(step - 1).wait_send()

        ex, ey, ez = efield[0], efield[1], efield[2]
        next_y = jnp.concatenate([ey[ny:], e_halo[step, 0]], axis=0)
        next_z = jnp.concatenate([ez[ny:], e_halo[step, 1]], axis=0)
        h_ref[1] = hfield[1] - COURANT * ((ahead_z(ex) - ex) - (next_z - ez))
        h_ref[2] = hfield[2] - COURANT * ((next_y - ey) - (ahead_y(ex) - ex))

        @pl.when(not_last)
        def _():
            h_copy(step).start()

        h_ref[0] = hfield[0] - COURANT * ((ahead_y(ez) - ez) - (ahead_z(ey) - ey))

    def electric(efield, density, step):
        @pl.when(not_first)
        def _():
            h_copy(step).wait_recv()
            e_copy(e_in, step).wait_send()

        hx, hy, hz = h_ref[0], h_ref[1], h_ref[2]
        prev_y = jnp.concatenate([h_halo[step, 0], hy[: rows - ny]], axis=0)
        prev_z = jnp.concatenate([h_halo[step, 1], hz[: rows - ny]], axis=0)
        keep, drive = keep_ref[...], drive_ref[...]
        ex, ey, ez = efield[0], efield[1], efield[2]
        curl_y = (hx - behind_z(hx)) - (hz - prev_z)
        e_ref[1] = keep * ey + drive * (curl_y - density[1])
        curl_z = (hy - prev_y) - (hx - behind_y(hx))
        e_ref[2] = keep * ez + drive * (curl_z - density[2])
        if step + 1 < STEPS:

            @pl.when(not_first)
            def _():
                e_copy(e_ref, step + 1).start()

        curl_x = (hz - behind_y(hz)) - (hy - behind_z(hy))
        e_ref[0] = keep * ex + drive * (curl_x - density[0])

    chunk = 512

    def gather_cells(efield):
        high, low = split(efield.reshape(3 * rows, nz))
        for start in range(0, slots, chunk):
            part = pl.ds(start, chunk)
            onehot = ohz_ref[:, part]
            picked = dot(high, onehot) + dot(low, onehot)
            mask = ohr_ref[:, part].astype(F32)
            for c in range(3):
                eg_ref[c : c + 1, part] = jnp.sum(
                    picked[c * rows : (c + 1) * rows] * mask, axis=0, keepdims=True
                )

    def scatter_density(index):
        b = as_rows(index)
        e = [eg_ref[c : c + 1, :] for c in range(3)]
        m = [m_ref[i : i + 1, :] for i in range(6)]
        values = (
            b[3:4] + m[0] * e[0] + m[1] * e[1] + m[2] * e[2],
            b[4:5] + m[1] * e[0] + m[3] * e[1] + m[4] * e[2],
            b[5:6] + m[2] * e[0] + m[4] * e[1] + m[5] * e[2],
        )
        for c in range(3):
            high = values[c].astype(BF16).astype(F32)
            for i, value in enumerate((high, values[c] - high)):
                tile = jnp.broadcast_to(value, (16, slots)).astype(BF16)
                place = (i * 3 + c) * rows
                spread_ref[place : place + rows, :] = ohr_ref[...] * jnp.concatenate(
                    [tile] * (rows // 16), axis=0
                )
        total = dot_nt(spread_ref[...], ohz_ref[...])
        total = total[: 3 * rows] + total[3 * rows :]
        return [total[c * rows : (c + 1) * rows] for c in range(3)]

    def start_messages(step):
        for k in range(n):
            msg_out[2 + step, k] = bout_ref[k] + eg_ref[:, k * cap : (k + 1) * cap]
        send_messages(2 + step)

    relative = jnp.bitwise_xor(seg_owner[...], me)
    member = (iota((n, seg), 0) == relative).astype(F32)
    block = min(seg, 256)
    before = (iota((block, block), 0) < iota((block, block), 1)).astype(F32).astype(BF16)
    ahead_count = jnp.zeros((n, 1), F32)
    ranks = []
    for start in range(0, seg, block):
        part = member[:, start : start + block]
        count = dot(part.astype(BF16), before) + ahead_count
        ranks.append(jnp.sum(count * part, axis=0, keepdims=True))
        ahead_count = ahead_count + jnp.sum(part, axis=1, keepdims=True)
    rank = jnp.concatenate(ranks, axis=1).astype(jnp.int32)
    rank_ref[...] = (iota((cap, seg), 0) == rank).astype(F32).astype(BF16)
    memb_ref[...] = (iota((n * 8, seg), 0) // 8 == relative).astype(F32)
    cell = seg_cell[...]
    cell_row = (cell // nz).astype(F32)
    cell_z = (cell % nz).astype(F32)
    msg_out[0] = to_slots(
        jnp.concatenate([cell_row, cell_z, jnp.zeros((6, seg), F32)], axis=0)
    )

    pl.semaphore_wait(barrier, n - 1)

    send_messages(0)

    @pl.when(not_first)
    def _():
        e_copy(e_in, 0).start()

    send_volt(v_in[...], 0)

    @pl.when(last)
    def _():
        e_halo[...] = jnp.zeros_like(e_halo)
        v_edge[...] = jnp.zeros_like(v_edge)

    @pl.when(first)
    def _():
        h_halo[...] = jnp.zeros_like(h_halo)
        i_edge[...] = jnp.zeros_like(i_edge)

    eg_ref[...] = jnp.zeros_like(eg_ref)

    for c in range(3):
        lc_ref[c] = times(induct[...], couple[c])
    quad = [jnp.sum(couple[a] * lc_ref[b], axis=0, keepdims=True) for a, b in PAIRS]
    msg_out[1] = to_slots(jnp.concatenate(quad + [jnp.zeros((2, seg), F32)], axis=0))
    send_messages(1)

    pending_current(i_in[...], v_in[...], 0)

    loss = mat_sigma[...] / (2.0 * mat_eps[...])
    keep_table = (1.0 - loss) / (1.0 + loss)
    drive_table = COURANT / (mat_eps[...] * (1.0 + loss))
    keep = jnp.zeros((rows, nz), F32)
    drive = jnp.zeros((rows, nz), F32)
    for i in range(mat_eps.shape[1]):
        here = material[...] == i
        keep = jnp.where(here, keep_table[:, i : i + 1], keep)
        drive = jnp.where(here, drive_table[:, i : i + 1], drive)
    keep_ref[...] = keep
    drive_ref[...] = drive

    wait_messages(0)
    cells = as_rows(0).astype(jnp.int32)
    ohr_ref[...] = (iota((rows, slots), 0) == cells[0:1]).astype(F32).astype(BF16)
    ohz_ref[...] = (iota((nz, slots), 0) == cells[1:2]).astype(F32).astype(BF16)

    gather_cells(e_in[...])
    start_messages(0)
    magnetic(e_in[...], h_in[...], 0)
    wait_messages(1)
    m_ref[...] = as_rows(1)

    for step in range(STEPS):
        wait_messages(2 + step)
        seen = from_slots(msg_in[2 + step])
        current = (
            j_ref[...]
            + lc_ref[0] * seen[0:1]
            + lc_ref[1] * seen[1:2]
            + lc_ref[2] * seen[2:3]
        )
        i_ref[...] = current
        i_out[step] = pack_edge(current[:, seg - 1 : seg])

        @pl.when(not_last)
        def _():
            i_copy(step).start()

        density = scatter_density(2 + step)

        @pl.when(not_first)
        def _():
            i_copy(step).wait_recv()

        volt = v_in[...] if step == 0 else v_ref[...]
        current = i_ref[...]
        edge = unpack_edge(i_edge[step])
        behind = jnp.where(seg_lane == 0, edge, pltpu.roll(current, 1, 1)) * link_behind
        volt = volt - times(capac[...], current - behind)
        v_ref[...] = volt
        if step + 1 < STEPS:
            send_volt(volt, step + 1)
        electric(e_in[...] if step == 0 else e_ref[...], density, step)
        if step + 1 < STEPS:
            gather_cells(e_ref[...])
            pending_current(i_ref[...], v_ref[...], step + 1)
            start_messages(step + 1)
            magnetic(e_ref[...], h_ref[...], step + 1)

    for index in range(STEPS + 2):
        wait_sent(index)

    @pl.when(not_last)
    def _():
        h_copy(STEPS - 1).wait_send()
        for step in range(STEPS):
            i_copy(step).wait_send()

    @pl.when(not_first)
    def _():
        for step in range(STEPS):
            v_copy(step).wait_send()


def per_device(
    n,
    efield,
    hfield,
    material,
    mat_eps,
    mat_sigma,
    seg_owner,
    seg_cell,
    chain_start,
    couple,
    voltage,
    current,
    induct_step,
    capac_step,
):
    _, nx, ny, nz = efield.shape
    rows = nx * ny
    cond, seg = voltage.shape
    cap = -(-(2 * seg // n) // LANES) * LANES
    edge = -(-cond // LANES) * LANES
    slots = n * cap
    dma = pltpu.SemaphoreType.DMA
    scratch = [
        pltpu.VMEM((rows, nz), F32),
        pltpu.VMEM((rows, nz), F32),
        pltpu.VMEM((n * 8, seg), F32),
        pltpu.VMEM((cap, seg), BF16),
        pltpu.VMEM((3, cond, seg), F32),
        pltpu.VMEM((cond, seg), F32),
        pltpu.VMEM((nz, slots), BF16),
        pltpu.VMEM((rows, slots), BF16),
        pltpu.VMEM((6 * rows, slots), BF16),
        pltpu.VMEM((8, slots), F32),
        pltpu.VMEM((8, slots), F32),
        pltpu.VMEM((n, 8, cap), F32),
        pltpu.VMEM((STEPS + 2, n, 8, cap), F32),
        pltpu.VMEM((STEPS + 2, n, 8, cap), F32),
        pltpu.VMEM((STEPS, 2, ny, nz), F32),
        pltpu.VMEM((STEPS, 2, ny, nz), F32),
        pltpu.VMEM((STEPS, 8, edge), F32),
        pltpu.VMEM((STEPS, 8, edge), F32),
        pltpu.VMEM((STEPS, 8, edge), F32),
        pltpu.VMEM((STEPS, 8, edge), F32),
        dma((STEPS + 2,)),
        dma((STEPS + 2,)),
    ] + [dma((STEPS,))] * 8
    vmem = pl.BlockSpec(memory_space=pltpu.VMEM)
    out = pl.pallas_call(
        functools.partial(kernel, n, ny),
        out_shape=(
            jax.ShapeDtypeStruct((3, rows, nz), F32),
            jax.ShapeDtypeStruct((3, rows, nz), F32),
            jax.ShapeDtypeStruct((cond, seg), F32),
            jax.ShapeDtypeStruct((cond, seg), F32),
        ),
        in_specs=[vmem] * 13,
        out_specs=(vmem,) * 4,
        scratch_shapes=scratch,
        compiler_params=pltpu.CompilerParams(
            collective_id=0, has_side_effects=True, vmem_limit_bytes=48 * 1024 * 1024
        ),
        name="leapfrog",
    )(
        efield.reshape(3, rows, nz),
        hfield.reshape(3, rows, nz),
        material.reshape(rows, nz),
        mat_eps.reshape(1, -1),
        mat_sigma.reshape(1, -1),
        seg_owner.reshape(1, seg),
        seg_cell.reshape(1, seg),
        chain_start.reshape(1, seg),
        couple,
        voltage,
        current,
        induct_step,
        capac_step,
    )
    return (
        out[0].reshape(efield.shape),
        out[1].reshape(hfield.shape),
        out[2],
        out[3],
    )


def solution(mesh):
    placed = (
        P(None, ("groups", "gx"), None, None),
        P(None, ("groups", "gx"), None, None),
        P(("groups", "gx"), None, None),
        P(),
        P(),
        P(("groups", "gx"), None),
        P(("groups", "gx")),
        P(("groups", "gx")),
        P(None, None, ("groups", "gx")),
        P(None, ("groups", "gx")),
        P(None, ("groups", "gx")),
        P(),
        P(),
    )
    return jax.shard_map(
        functools.partial(per_device, mesh.shape["gx"]),
        mesh=mesh,
        in_specs=placed,
        out_specs=(
            P(None, ("groups", "gx"), None, None),
            P(None, ("groups", "gx"), None, None),
            P(None, ("groups", "gx")),
            P(None, ("groups", "gx")),
        ),
        check_vma=False,
    )
```

profile of v0, /device:TPU:0, one launch (start us, length us, event | category | flops | bytes accessed | tf_op | source)
XLA Modules:
  0.0 63.5 jit_solution(173670442834393222)
XLA Ops:
  0.6 0.0 copy-start.10
  0.6 0.0 copy-start.9
  0.7 0.0 copy-start.8
  0.7 0.0 copy-start.11
  0.7 0.0 copy-start.12
  0.7 0.6 %copy-done.10 = s32[1024]{0:T(1024)S(1)} copy-done((s32[1024]{0:T(1024)S(1)}, s32[1024]{0:T(1024)}, u32[]{:S(2)}) %copy-start.10) | copy-done | bytes 4120
  1.3 0.0 copy-done.9
  1.3 0.0 copy-done.8
  1.4 0.0 copy-done.11
  1.4 0.0 copy-done.12
  1.4 0.0 copy-start
  1.4 1.1 %copy-done = f32[3,64,1024]{2,1,0:T(8,128)S(1)} copy-done((f32[3,64,1024]{2,1,0:T(8,128)S(1)}, f32[3,64,1024]{2,1,0:T(8,128)}, u32[]{:S(2)}) %copy-start) | copy-done | bytes 786456
  2.5 1.0 %copy-done.1 = f32[3,2,64,256]{3,2,1,0:T(8,128)S(1)} copy-done((f32[3,2,64,256]{3,2,1,0:T(8,128)S(1)}, f32[3,2,64,256]{3,2,1,0:T(8,128)}, u32[]{:S(2)}) %copy-start.1) | copy-done | bytes 393240
  3.5 1.0 %copy-done.2 = f32[3,2,64,256]{3,2,1,0:T(8,128)S(1)} copy-done((f32[3,2,64,256]{3,2,1,0:T(8,128)S(1)}, f32[3,2,64,256]{3,2,1,0:T(8,128)}, u32[]{:S(2)}) %copy-start.2) | copy-done | bytes 393240
  4.5 0.9 %copy-done.3 = f32[64,1024]{1,0:T(8,128)S(1)} copy-done((f32[64,1024]{1,0:T(8,128)S(1)}, f32[64,1024]{1,0:T(8,128)}, u32[]{:S(2)}) %copy-start.3) | copy-done | bytes 262168
  5.4 0.9 %copy-done.4 = f32[64,1024]{1,0:T(8,128)S(1)} copy-done((f32[64,1024]{1,0:T(8,128)S(1)}, f32[64,1024]{1,0:T(8,128)}, u32[]{:S(2)}) %copy-start.4) | copy-done | bytes 262168
  6.4 0.9 %copy-done.5 = s32[2,64,256]{2,1,0:T(8,128)S(1)} copy-done((s32[2,64,256]{2,1,0:T(8,128)S(1)}, s32[2,64,256]{2,1,0:T(8,128)}, u32[]{:S(2)}) %copy-start.5) | copy-done | bytes 131096
  7.3 0.8 %copy-done.6 = f32[64,64]{1,0:T(8,128)S(1)} copy-done((f32[64,64]{1,0:T(8,128)S(1)}, f32[64,64]{1,0:T(8,128)}, u32[]{:S(2)}) %copy-start.6) | copy-done | bytes 16408
  8.1 0.8 %copy-done.7 = f32[64,64]{1,0:T(8,128)S(1)} copy-done((f32[64,64]{1,0:T(8,128)S(1)}, f32[64,64]{1,0:T(8,128)}, u32[]{:S(2)}) %copy-start.7) | copy-done | bytes 16408
  8.8 51.8 %leapfrog.1 = (f32[3,128,256]{2,1,0:T(8,128)S(1)}, f32[3,128,256]{2,1,0:T(8,128)S(1)}, f32[64,1024]{1,0:T(8,128)S(1)}, f32[64,1024]{1,0:T(8,128)S(1)}) custom-call(f32[3,128,256]{2,1,0:T(8,128)S(1)} %bitcast.12, f32[3,128,256]{2,1,0:T(8,128)S(1)} %bitcast.13, s32[128,256]{1,0:T(8,128)S(1)} %bitcast.14, f32[1,16]{1,0:T(1,128)S(1)} %bitcast.18, ...), custom_call_target="tpu_custom_call" | custom-call | tf_op jit(solution)/shard_map/leapfrog/pallas_call | solution.py:486
  60.6 0.7 %copy.21 = f32[3,2,64,256]{3,2,1,0:T(8,128)} copy(f32[3,2,64,256]{3,2,1,0:T(8,128)S(1)} %bitcast.11) | data formatting | bytes 786432
  61.4 0.7 %copy.22 = f32[3,2,64,256]{3,2,1,0:T(8,128)} copy(f32[3,2,64,256]{3,2,1,0:T(8,128)S(1)} %bitcast.10) | data formatting | bytes 786432
  62.1 0.7 %copy.23 = f32[64,1024]{1,0:T(8,128)} copy(f32[64,1024]{1,0:T(8,128)S(1)} %get-tuple-element.18) | data formatting | bytes 524288
  62.8 0.7 %copy.24 = f32[64,1024]{1,0:T(8,128)} copy(f32[64,1024]{1,0:T(8,128)S(1)} %get-tuple-element.19) | data formatting | bytes 524288
  (7 shorter events, 0.0 us)
Async XLA Ops:
  0.6 0.7 %copy-start.10 = (s32[1024]{0:T(1024)S(1)}, s32[1024]{0:T(1024)}, u32[]{:S(2)}) copy-start(s32[1024]{0:T(1024)} %param.20) | copy-start | bytes 12292
  0.6 0.7 %copy-start.9 = (s32[1024]{0:T(1024)S(1)}, s32[1024]{0:T(1024)}, u32[]{:S(2)}) copy-start(s32[1024]{0:T(1024)} %param.19) | copy-start | bytes 12292
  0.7 0.7 %copy-start.8 = (s32[1024,1]{0,1:T(1,128)S(1)}, s32[1024,1]{0,1:T(1,128)}, u32[]{:S(2)}) copy-start(s32[1024,1]{0,1:T(1,128)} %param.18) | copy-start | bytes 12292
  0.7 0.7 %copy-start.11 = (f32[16]{0:T(128)S(1)}, f32[16]{0:T(128)}, u32[]{:S(2)}) copy-start(f32[16]{0:T(128)} %param.16) | copy-start | bytes 196
  0.7 0.7 %copy-start.12 = (f32[16]{0:T(128)S(1)}, f32[16]{0:T(128)}, u32[]{:S(2)}) copy-start(f32[16]{0:T(128)} %param.17) | copy-start | bytes 196
  1.4 1.1 %copy-start = (f32[3,64,1024]{2,1,0:T(8,128)S(1)}, f32[3,64,1024]{2,1,0:T(8,128)}, u32[]{:S(2)}) copy-start(f32[3,64,1024]{2,1,0:T(8,128)} %couple.1) | copy-start | bytes 2359300
  2.5 1.0 %copy-start.1 = (f32[3,2,64,256]{3,2,1,0:T(8,128)S(1)}, f32[3,2,64,256]{3,2,1,0:T(8,128)}, u32[]{:S(2)}) copy-start(f32[3,2,64,256]{3,2,1,0:T(8,128)} %param.13) | copy-start | bytes 1179652
  3.5 1.0 %copy-start.2 = (f32[3,2,64,256]{3,2,1,0:T(8,128)S(1)}, f32[3,2,64,256]{3,2,1,0:T(8,128)}, u32[]{:S(2)}) copy-start(f32[3,2,64,256]{3,2,1,0:T(8,128)} %param.14) | copy-start | bytes 1179652
  4.5 0.9 %copy-start.3 = (f32[64,1024]{1,0:T(8,128)S(1)}, f32[64,1024]{1,0:T(8,128)}, u32[]{:S(2)}) copy-start(f32[64,1024]{1,0:T(8,128)} %v_in.1) | copy-start | bytes 786436
  5.4 0.9 %copy-start.4 = (f32[64,1024]{1,0:T(8,128)S(1)}, f32[64,1024]{1,0:T(8,128)}, u32[]{:S(2)}) copy-start(f32[64,1024]{1,0:T(8,128)} %i_in.1) | copy-start | bytes 786436
  6.4 0.9 %copy-start.5 = (s32[2,64,256]{2,1,0:T(8,128)S(1)}, s32[2,64,256]{2,1,0:T(8,128)}, u32[]{:S(2)}) copy-start(s32[2,64,256]{2,1,0:T(8,128)} %param.15) | copy-start | bytes 393220
  7.3 0.8 %copy-start.6 = (f32[64,64]{1,0:T(8,128)S(1)}, f32[64,64]{1,0:T(8,128)}, u32[]{:S(2)}) copy-start(f32[64,64]{1,0:T(8,128)} %induct.1) | copy-start | bytes 49156
  8.1 0.8 %copy-start.7 = (f32[64,64]{1,0:T(8,128)S(1)}, f32[64,64]{1,0:T(8,128)}, u32[]{:S(2)}) copy-start(f32[64,64]{1,0:T(8,128)} %capac.1) | copy-start | bytes 49156
where the time goes:
time: 64 us; the launch traced here: 63.5 us
  Pallas kernels  51.8 us (81%)
  local copies, waits for them, and re-layouts  11 us (17%)
  between operations  0.7 us (1%)
    pallas_call x1, Pallas kernels, per_device(): pl.pallas_call(functools.partial(kernel, n, ny), out_shape=(jax.ShapeDtyp...  51.8 us
    unnamed x30, local copies, waits for them, and re-layouts  11 us

commit v1 on v0

--- a/solution.py
+++ b/solution.py
@@ -36,57 +36,58 @@
 def kernel(
     n,
     ny,
-    e_in,
-    h_in,
-    material,
-    mat_eps,
-    mat_sigma,
-    seg_owner,
-    seg_cell,
-    chain_start,
-    couple,
-    v_in,
-    i_in,
-    induct,
-    capac,
-    e_ref,
-    h_ref,
-    v_ref,
-    i_ref,
-    keep_ref,
-    drive_ref,
-    memb_ref,
-    rank_ref,
-    lc_ref,
-    j_ref,
-    ohz_ref,
-    ohr_ref,
-    spread_ref,
-    m_ref,
-    eg_ref,
-    bout_ref,
-    msg_out,
-    msg_in,
-    e_halo,
-    h_halo,
-    v_out,
-    v_edge,
-    i_out,
-    i_edge,
-    msg_ssem,
-    msg_rsem,
-    e_ssem,
-    e_rsem,
-    h_ssem,
-    h_rsem,
-    v_ssem,
-    v_rsem,
-    i_ssem,
-    i_rsem,
+    *refs,
 ):
+    sources, refs = refs[:13], refs[13:]
+    (
+        e_ref,
+        h_ref,
+        v_ref,
+        i_ref,
+        material,
+        mat_eps,
+        mat_sigma,
+        seg_owner,
+        seg_cell,
+        chain_start,
+        couple,
+        induct,
+        capac,
+        load_sem,
+        keep_ref,
+        drive_ref,
+        memb_ref,
+        rank_ref,
+        lc_ref,
+        j_ref,
+        ohz_ref,
+        ohr_ref,
+        spread_ref,
+        m_ref,
+        eg_ref,
+        bout_ref,
+        msg_out,
+        msg_in,
+        e_halo,
+        h_halo,
+        v_out,
+        v_edge,
+        i_out,
+        i_edge,
+        msg_ssem,
+        msg_rsem,
+        e_ssem,
+        e_rsem,
+        h_ssem,
+        h_rsem,
+        v_ssem,
+        v_rsem,
+        i_ssem,
+        i_rsem,
+    ) = refs
     me = lax.axis_index("gx")
-    _, rows, nz = e_in.shape
-    cond, seg = v_in.shape
+    _, rows, nz = e_ref.shape
+    cond, seg = v_ref.shape
     cap = msg_in.shape[-1]
     slots = n * cap
     first, last = me == 0, me == n - 1
@@ -101,6 +102,29 @@
         return result
 
     partners = [partner(k) for k in range(n)]
+
+    places = {
+        "seg_owner": (5, seg_owner),
+        "seg_cell": (6, seg_cell),
+        "efield": (0, e_ref),
+        "chain_start": (7, chain_start),
+        "voltage": (9, v_ref),
+        "induct": (11, induct),
+        "couple": (8, couple),
+        "current": (10, i_ref),
+        "mat_eps": (3, mat_eps),
+        "mat_sigma": (4, mat_sigma),
+        "material": (2, material),
+        "hfield": (1, h_ref),
+        "capac": (12, capac),
+    }
+
+    def load(name):
+        index, target = places[name]
+        return pltpu.make_async_copy(sources[index], target, load_sem.at[index])
+
+    for name in places:
+        load(name).start()
 
     barrier = pltpu.get_barrier_semaphore()
     for k in range(1, n):
@@ -139,9 +163,9 @@
             device_id_type=MESH,
         )
 
-    def e_copy(source, step):
+    def e_copy(step):
         return to_neighbour(
-            source.at[pl.ds(1, 2), pl.ds(0, ny)], e_halo, e_ssem, e_rsem, step, -1
+            e_ref.at[pl.ds(1, 2), pl.ds(0, ny)], e_halo, e_ssem, e_rsem, step, -1
         )
 
     def h_copy(step):
@@ -154,6 +178,29 @@
 
     def i_copy(step):
         return to_neighbour(i_out.at[step], i_edge, i_ssem, i_rsem, step, 1)
+
+    load("seg_owner").wait()
+    load("seg_cell").wait()
+    relative = jnp.bitwise_xor(seg_owner[...], me)
+    member = (iota((n, seg), 0) == relative).astype(F32)
+    block = min(seg, 256)
+    before = (iota((block, block), 0) < iota((block, block), 1)).astype(F32).astype(BF16)
+    ahead_count = jnp.zeros((n, 1), F32)
+    ranks = []
+    for start in range(0, seg, block):
+        part = member[:, start : start + block]
+        count = dot(part.astype(BF16), before) + ahead_count
+        ranks.append(jnp.sum(count * part, axis=0, keepdims=True))
+        ahead_count = ahead_count + jnp.sum(part, axis=1, keepdims=True)
+    rank = jnp.concatenate(ranks, axis=1).astype(jnp.int32)
+    rank_ref[...] = (iota((cap, seg), 0) == rank).astype(F32).astype(BF16)
+    memb_ref[...] = (iota((n * 8, seg), 0) // 8 == relative).astype(F32)
+    cell = seg_cell[...]
+    cell_row = (cell // nz).astype(F32)
+    cell_z = (cell % nz).astype(F32)
+    load("efield").wait()
+    load("chain_start").wait()
+    load("voltage").wait()
 
     link_behind = 1.0 - chain_start[...].astype(F32)
     eye = iota((cond, v_edge.shape[-1]), 0) == iota((cond, v_edge.shape[-1]), 1)
@@ -225,7 +272,7 @@
     def magnetic(efield, hfield, step):
         @pl.when(not_last)
         def _():
-            e_copy(e_in, step).wait_recv()
+            e_copy(step).wait_recv()
 
         if step > 0:
 
@@ -249,7 +296,7 @@
         @pl.when(not_first)
         def _():
             h_copy(step).wait_recv()
-            e_copy(e_in, step).wait_send()
+            e_copy(step).wait_send()
 
         hx, hy, hz = h_ref[0], h_ref[1], h_ref[2]
         prev_y = jnp.concatenate([h_halo[step, 0], hy[: rows - ny]], axis=0)
@@ -264,7 +311,7 @@
 
             @pl.when(not_first)
             def _():
-                e_copy(e_ref, step + 1).start()
+                e_copy(step + 1).start()
 
         curl_x = (hz - behind_y(hz)) - (hy - behind_z(hy))
         e_ref[0] = keep * ex + drive * (curl_x - density[0])
@@ -309,23 +356,6 @@
             msg_out[2 + step, k] = bout_ref[k] + eg_ref[:, k * cap : (k + 1) * cap]
         send_messages(2 + step)
 
-    relative = jnp.bitwise_xor(seg_owner[...], me)
-    member = (iota((n, seg), 0) == relative).astype(F32)
-    block = min(seg, 256)
-    before = (iota((block, block), 0) < iota((block, block), 1)).astype(F32).astype(BF16)
-    ahead_count = jnp.zeros((n, 1), F32)
-    ranks = []
-    for start in range(0, seg, block):
-        part = member[:, start : start + block]
-        count = dot(part.astype(BF16), before) + ahead_count
-        ranks.append(jnp.sum(count * part, axis=0, keepdims=True))
-        ahead_count = ahead_count + jnp.sum(part, axis=1, keepdims=True)
-    rank = jnp.concatenate(ranks, axis=1).astype(jnp.int32)
-    rank_ref[...] = (iota((cap, seg), 0) == rank).astype(F32).astype(BF16)
-    memb_ref[...] = (iota((n * 8, seg), 0) // 8 == relative).astype(F32)
-    cell = seg_cell[...]
-    cell_row = (cell // nz).astype(F32)
-    cell_z = (cell % nz).astype(F32)
     msg_out[0] = to_slots(
         jnp.concatenate([cell_row, cell_z, jnp.zeros((6, seg), F32)], axis=0)
     )
@@ -336,9 +366,9 @@
 
     @pl.when(not_first)
     def _():
-        e_copy(e_in, 0).start()
-
-    send_volt(v_in[...], 0)
+        e_copy(0).start()
+
+    send_volt(v_ref[...], 0)
 
     @pl.when(last)
     def _():
@@ -352,13 +382,19 @@
 
     eg_ref[...] = jnp.zeros_like(eg_ref)
 
+    load("induct").wait()
+    load("couple").wait()
     for c in range(3):
         lc_ref[c] = times(induct[...], couple[c])
     quad = [jnp.sum(couple[a] * lc_ref[b], axis=0, keepdims=True) for a, b in PAIRS]
     msg_out[1] = to_slots(jnp.concatenate(quad + [jnp.zeros((2, seg), F32)], axis=0))
     send_messages(1)
 
-    pending_current(i_in[...], v_in[...], 0)
+    load("current").wait()
+    pending_current(i_ref[...], v_ref[...], 0)
+
+    for name in ("mat_eps", "mat_sigma", "material", "hfield", "capac"):
+        load(name).wait()
 
     loss = mat_sigma[...] / (2.0 * mat_eps[...])
     keep_table = (1.0 - loss) / (1.0 + loss)
@@ -377,9 +413,9 @@
     ohr_ref[...] = (iota((rows, slots), 0) == cells[0:1]).astype(F32).astype(BF16)
     ohz_ref[...] = (iota((nz, slots), 0) == cells[1:2]).astype(F32).astype(BF16)
 
-    gather_cells(e_in[...])
+    gather_cells(e_ref[...])
     start_messages(0)
-    magnetic(e_in[...], h_in[...], 0)
+    magnetic(e_ref[...], h_ref[...], 0)
     wait_messages(1)
     m_ref[...] = as_rows(1)
 
@@ -405,7 +441,7 @@
         def _():
             i_copy(step).wait_recv()
 
-        volt = v_in[...] if step == 0 else v_ref[...]
+        volt = v_ref[...]
         current = i_ref[...]
         edge = unpack_edge(i_edge[step])
         behind = jnp.where(seg_lane == 0, edge, pltpu.roll(current, 1, 1)) * link_behind
@@ -413,7 +449,7 @@
         v_ref[...] = volt
         if step + 1 < STEPS:
             send_volt(volt, step + 1)
-        electric(e_in[...] if step == 0 else e_ref[...], density, step)
+        electric(e_ref[...], density, step)
         if step + 1 < STEPS:
             gather_cells(e_ref[...])
             pending_current(i_ref[...], v_ref[...], step + 1)
@@ -433,6 +469,14 @@
     def _():
         for step in range(STEPS):
             v_copy(step).wait_send()
+
+
+def write_out(*refs):
+    copies = [pltpu.make_async_copy(refs[i], refs[4 + i], refs[8].at[i]) for i in range(4)]
+    for copy in copies:
+        copy.start()
+    for copy in copies:
+        copy.wait()
 
 
 def per_device(
@@ -459,6 +503,16 @@
     slots = n * cap
     dma = pltpu.SemaphoreType.DMA
     scratch = [
+        pltpu.VMEM((rows, nz), jnp.int32),
+        pltpu.VMEM((1, mat_eps.shape[0]), F32),
+        pltpu.VMEM((1, mat_eps.shape[0]), F32),
+        pltpu.VMEM((1, seg), jnp.int32),
+        pltpu.VMEM((1, seg), jnp.int32),
+        pltpu.VMEM((1, seg), jnp.int32),
+        pltpu.VMEM((3, cond, seg), F32),
+        pltpu.VMEM((cond, cond), F32),
+        pltpu.VMEM((cond, cond), F32),
+        dma((13,)),
         pltpu.VMEM((rows, nz), F32),
         pltpu.VMEM((rows, nz), F32),
         pltpu.VMEM((n * 8, seg), F32),
@@ -483,6 +537,7 @@
         dma((STEPS + 2,)),
     ] + [dma((STEPS,))] * 8
     vmem = pl.BlockSpec(memory_space=pltpu.VMEM)
+    hbm = pl.BlockSpec(memory_space=pltpu.HBM)
     out = pl.pallas_call(
         functools.partial(kernel, n, ny),
         out_shape=(
@@ -491,11 +546,11 @@
             jax.ShapeDtypeStruct((cond, seg), F32),
             jax.ShapeDtypeStruct((cond, seg), F32),
         ),
-        in_specs=[vmem] * 13,
+        in_specs=[hbm] * 13,
         out_specs=(vmem,) * 4,
         scratch_shapes=scratch,
         compiler_params=pltpu.CompilerParams(
-            collective_id=0, has_side_effects=True, vmem_limit_bytes=48 * 1024 * 1024
+            collective_id=0, has_side_effects=True, vmem_limit_bytes=56 * 1024 * 1024
         ),
         name="leapfrog",
     )(
@@ -513,6 +568,15 @@
         induct_step,
         capac_step,
     )
+    out = pl.pallas_call(
+        write_out,
+        out_shape=tuple(jax.ShapeDtypeStruct(x.shape, x.dtype) for x in out),
+        in_specs=[hbm] * 4,
+        out_specs=(hbm,) * 4,
+        scratch_shapes=[dma((4,))],
+        compiler_params=pltpu.CompilerParams(vmem_limit_bytes=56 * 1024 * 1024),
+        name="write_out",
+    )(*out)
     return (
         out[0].reshape(efield.shape),
         out[1].reshape(hfield.shape),

time: 64 us -> 95.1 us (1.49)
  Pallas kernels: 51.8 us -> 94.2 us
  local copies, waits for them, and re-layouts: 11 us -> 0 us
    pallas_call x0 -> x1, Pallas kernels: none -> 40.8 us  [per_device(): pl.pallas_call(write_out, out_shape=tuple((jax.ShapeDtypeStruct(x.shape,...]
    unnamed x30 -> x0, local copies, waits for them, and re-layouts: 11 us -> none
    pallas_call x1, Pallas kernels: 51.8 us -> 53.3 us  [per_device(): pl.pallas_call(functools.partial(kernel, n, ny), out_shape=(jax.ShapeDtyp...]
where the time goes in v1:
time: 95.1 us; the launch traced here: 95 us
  Pallas kernels  94.2 us (99%)
    pallas_call x1, Pallas kernels, per_device(): pl.pallas_call(functools.partial(kernel, n, ny), out_shape=(jax.ShapeDtyp...  53.3 us
    pallas_call x1, Pallas kernels, per_device(): pl.pallas_call(write_out, out_shape=tuple((jax.ShapeDtypeStruct(x.shape,...  40.8 us

profile of v1, /device:TPU:0, one launch (start us, length us, event | category | flops | bytes accessed | tf_op | source)
XLA Modules:
  0.0 95.0 jit_solution(16880445444077516152)
XLA Ops:
  0.6 53.3 %leapfrog.1 = (f32[3,128,256]{2,1,0:T(8,128)}, f32[3,128,256]{2,1,0:T(8,128)}, f32[64,1024]{1,0:T(8,128)}, f32[64,1024]{1,0:T(8,128)}) custom-call(f32[3,128,256]{2,1,0:T(8,128)} %bitcast.10, f32[3,128,256]{2,1,0:T(8,128)} %bitcast.11, s32[128,256]{1,0:T(8,128)} %bitcast.12, f32[1,16]{1,0:T(1,128)} %bitcast.16, f32[1,16]{1,0:T(1,128)} %bitcast.17, ...), custom_call_target="tpu_custom_call" | custom-call | tf_op jit(solution)/shard_map/leapfrog/pallas_call | solution.py:541
  54.0 40.8 %write_out.1 = (f32[3,128,256]{2,1,0:T(8,128)}, f32[3,128,256]{2,1,0:T(8,128)}, f32[64,1024]{1,0:T(8,128)}, f32[64,1024]{1,0:T(8,128)}) custom-call(f32[3,128,256]{2,1,0:T(8,128)} %get-tuple-element.12.refs_0_, f32[3,128,256]{2,1,0:T(8,128)} %get-tuple-element.13.refs_1_, f32[64,1024]{1,0:T(8,128)} %get-tuple-element.14.refs_2_, ...), custom_call_target="tpu_custom_call" | custom-call | tf_op jit(solution)/shard_map/write_out/pallas_call | solution.py:571

commit v2 on v1

--- a/solution.py
+++ b/solution.py
@@ -472,11 +472,15 @@
 
 
 def write_out(*refs):
-    copies = [pltpu.make_async_copy(refs[i], refs[4 + i], refs[8].at[i]) for i in range(4)]
-    for copy in copies:
-        copy.start()
-    for copy in copies:
-        copy.wait()
+    loads = [pltpu.make_async_copy(refs[i], refs[8 + i], refs[12].at[i]) for i in range(4)]
+    stores = [pltpu.make_async_copy(refs[8 + i], refs[4 + i], refs[13].at[i]) for i in range(4)]
+    for load in loads:
+        load.start()
+    for load, store in zip(loads, stores):
+        load.wait()
+        store.start()
+    for store in stores:
+        store.wait()
 
 
 def per_device(
@@ -573,7 +577,7 @@
         out_shape=tuple(jax.ShapeDtypeStruct(x.shape, x.dtype) for x in out),
         in_specs=[hbm] * 4,
         out_specs=(hbm,) * 4,
-        scratch_shapes=[dma((4,))],
+        scratch_shapes=[pltpu.VMEM(x.shape, x.dtype) for x in out] + [dma((4,))] * 2,
         compiler_params=pltpu.CompilerParams(vmem_limit_bytes=56 * 1024 * 1024),
         name="write_out",
     )(*out)

time: 95.1 us -> 56.4 us (0.59)
  Pallas kernels: 94.2 us -> 55.4 us
    pallas_call x1, Pallas kernels: 40.8 us -> 2.11 us  [per_device(): pl.pallas_call(write_out, out_shape=tuple((jax.ShapeDtypeStruct(x.shape,...]
where the time goes in v2:
time: 56.4 us; the launch traced here: 56.2 us
  Pallas kernels  55.4 us (98%)
  between operations  0.8 us (1%)
    pallas_call x1, Pallas kernels, per_device(): pl.pallas_call(functools.partial(kernel, n, ny), out_shape=(jax.ShapeDtyp...  53.3 us
    pallas_call x1, Pallas kernels, per_device(): pl.pallas_call(write_out, out_shape=tuple((jax.ShapeDtypeStruct(x.shape,...  2.11 us

profile of v2, /device:TPU:0, one launch (start us, length us, event | category | flops | bytes accessed | tf_op | source)
XLA Modules:
  0.0 56.2 jit_solution(4081815840771633241)
XLA Ops:
  0.6 53.3 %leapfrog.1 = (f32[3,128,256]{2,1,0:T(8,128)}, f32[3,128,256]{2,1,0:T(8,128)}, f32[64,1024]{1,0:T(8,128)}, f32[64,1024]{1,0:T(8,128)}) custom-call(f32[3,128,256]{2,1,0:T(8,128)} %bitcast.10, f32[3,128,256]{2,1,0:T(8,128)} %bitcast.11, s32[128,256]{1,0:T(8,128)} %bitcast.12, f32[1,16]{1,0:T(1,128)} %bitcast.16, f32[1,16]{1,0:T(1,128)} %bitcast.17, ...), custom_call_target="tpu_custom_call" | custom-call | tf_op jit(solution)/shard_map/leapfrog/pallas_call | solution.py:545
  54.0 2.1 %write_out.1 = (f32[3,128,256]{2,1,0:T(8,128)}, f32[3,128,256]{2,1,0:T(8,128)}, f32[64,1024]{1,0:T(8,128)}, f32[64,1024]{1,0:T(8,128)}) custom-call(f32[3,128,256]{2,1,0:T(8,128)} %get-tuple-element.12.refs_0_, f32[3,128,256]{2,1,0:T(8,128)} %get-tuple-element.13.refs_1_, f32[64,1024]{1,0:T(8,128)} %get-tuple-element.14.refs_2_, ...), custom_call_target="tpu_custom_call" | custom-call | tf_op jit(solution)/shard_map/write_out/pallas_call | solution.py:575
